TPU v7x, 256 devices: a whole 4x4x8 slice. The times are simulated.
256 devices in a mesh: fsdp: 64 (over x, z, core), rep: 4 (over y).
Axes of the slice: x: 4, y: 4, z: 8, core: 2. Of those that a mesh axis runs over, the one named last changes fastest.
Arguments:
- hidden_rows: bfloat16 [32768, 5120], P(('rep', 'fsdp')), parts along dimension 0, may hold values from -6 to 6
- queries: bfloat16 [32768, 4096], P(('rep', 'fsdp')), parts along dimension 0, may hold values from -6 to 6
- norm_gain: float32 [5120], replicated, may hold values from 0.1 to 1.9
- query_gain: float32 [128], replicated, may hold values from 0.5 to 12
- key_norm_gain: float32 [128], replicated, may hold values from 0.5 to 2
- key_matrix: bfloat16 [5120, 512], P('fsdp'), may hold values from -0.078125 to 0.078125
- value_matrix: bfloat16 [5120, 512], P('fsdp'), may hold values from -0.078125 to 0.078125
- lengths: int32 [256], P('rep'), parts along dimension 0, may hold values from 1 to 256, as said below
- owner: int32 [256], P('rep'), parts along dimension 0, may hold values from 0 to 63, as said below
Outputs:
- context: bfloat16 [32768, 4096], P(('rep', 'fsdp')), parts along dimension 0
There are 4 independent parts, one for each index of `rep`. A program takes and returns all parts, laid end to end along the dimension named above; an argument that names none is the same for every part. Nothing has to cross between parts.
Inputs may be any that keep to these rules, and one draw needn't show every extreme that they name: The lengths sum to 8192; one rollout has exactly 256 tokens. The rollouts of one owner hold at most 256 tokens together; some owner holds exactly 256.
All inputs are finite; a program needn't handle non-finite values.
Results may differ from a plain program's by a relative error of at most 0.012.
The roundings to bfloat16 on the way count: a program that leaves them out, or rounds other values in their place, can miss the bound.
Values may be sent and summed in bfloat16 or wider, within the bound.
No kernel may reach another device: no remote copies, remote signals or barrier semaphores. Data moves between devices by JAX's collectives and lax.ppermute only.
A program may use at most 128 MiB of HBM per device.

v0:
```python
import functools

import jax
import jax.numpy as jnp
import numpy as np
from jax import lax
from jax.experimental import pallas as pl
from jax.experimental.pallas import tpu as pltpu
from jax.sharding import Mesh, PartitionSpec as P

NX, NZ, NC = 4, 8, 2
NF = NX * NZ * NC
WIDTH = 5120
HEADS = 8
HEAD = 128
ROWS = 128
SHARD = WIDTH // NF
RNG = 8
HALO = 4
KROWS = RNG + HALO
QTOK = NF * RNG
KTOK = NF * KROWS
X_ORDER = (0, -1, 1, 2)
Z_ORDER = (0, -1, 1, -2, 2, -3, 3, 4)

eps = 1e-06
rope_base = 1000000.0
BF = jnp.bfloat16
F32 = jnp.float32


def shift(value, axis, size, by):
    return lax.ppermute(value, axis, [(i, (i + by) % size) for i in range(size)])


def rollout_starts(lengths, owner, tokens):
    index = jnp.arange(lengths.shape[0], dtype=jnp.int32)
    earlier = (owner[None, :] < owner[:, None]) | (owner[None, :] == owner[:, None]) & (
        index[None, :] < index[:, None]
    )
    offset = jnp.sum(jnp.where(earlier, lengths[None, :], 0), axis=1)
    return jnp.max(jnp.where(offset[None, :] <= tokens[:, None], offset[None, :], 0), axis=1)


def rope_tables(positions):
    half = HEAD // 2
    steps = jnp.arange(half, dtype=F32) * (2.0 / HEAD)
    inverse = jnp.power(F32(rope_base), -steps)
    angles = positions.astype(F32)[:, None] * inverse[None, :]
    cosine = jnp.cos(angles)
    sine = jnp.sin(angles)
    return (
        jnp.concatenate([cosine, cosine], axis=1),
        jnp.concatenate([-sine, sine], axis=1),
    )


def normed_rope(value, gain, cosine, sine):
    mean_square = jnp.mean(value * value, axis=-1, keepdims=True)
    value = value * lax.rsqrt(mean_square + eps) * gain
    return value * cosine + pltpu.roll(value, HEAD // 2, 1) * sine


def project_kernel(
    place, own, left, right, far_a, far_b, mine, other, gain, cosine, sine, out, weight, keep_k, keep_v, sem
):
    z, c = place[1], place[2]
    copies = []
    for k, by in enumerate(Z_ORDER):
        at = lax.rem(z + by + NZ, NZ)
        for which, core in ((mine, c), (other, 1 - c)):
            copies.append(
                pltpu.make_async_copy(
                    which.at[k], weight.at[:, at, core], sem.at[len(copies)]
                )
            )
    for copy in copies:
        copy.start()
    for copy in copies:
        copy.wait()
    w = weight[...].reshape(WIDTH, 2 * HEAD)
    for k in range(NX):
        x = (
            (own, left, right)[k][...]
            if k < 3
            else jnp.concatenate([far_a[...], far_b[...]], axis=0)
        )
        raw = jnp.dot(x, w, preferred_element_type=F32)
        rows = pl.ds(k * ROWS, ROWS)
        key = normed_rope(raw[:, :HEAD], gain[...], cosine[rows, :], sine[rows, :])
        keep_k[pl.ds(k, ROWS, stride=NX), :] = key
        keep_v[pl.ds(k, ROWS, stride=NX), :] = raw[:, HEAD:]
    out[0, : NX * HALO, :] = jnp.zeros((NX * HALO, 2 * HEAD), BF)
    for keep, lanes in ((keep_k, pl.ds(0, HEAD)), (keep_v, pl.ds(HEAD, HEAD))):
        out[0, NX * HALO :, lanes] = keep[: NX * RNG, :].astype(BF)
        for j in range(1, NZ * NC):
            start = NX * (RNG * j - HALO)
            out[j, :, lanes] = keep[start : start + NX * KROWS, :].astype(BF)


def prepare_kernel(q, gain, cosine, sine, out):
    value = q[...].astype(F32)
    out[...] = normed_rope(value, gain[...], cosine[...], sine[...]).astype(BF)


def attend_kernel(q, kv, token, start, key_token, out, bias, scores, probs):
    @pl.when(pl.program_id(0) == 0)
    def _():
        seen = (key_token[...] >= start[...]) & (key_token[...] <= token[...])
        bias[...] = jnp.where(seen, 0.0, -jnp.inf)

    keys = kv[:, :HEAD]
    values = kv[:, HEAD:]
    scores[...] = lax.dot_general(
        q[...], keys, (((1,), (1,)), ((), ())), preferred_element_type=F32
    )
    block = 64

    def body(i, carry):
        rows = pl.ds(pl.multiple_of(i * block, block), block)
        s = scores[rows, :] * (1.0 / np.sqrt(HEAD)).astype(np.float32) + bias[rows, :]
        top = jnp.max(s, axis=1, keepdims=True)
        weights = jnp.exp(s - top)
        total = jnp.sum(weights, axis=1, keepdims=True)
        probs[rows, :] = (weights / total).astype(BF)
        return carry

    lax.fori_loop(0, QTOK // block, body, 0)
    out[...] = jnp.dot(probs[...], values, preferred_element_type=F32).astype(BF)


def per_device(
    hidden_rows,
    queries,
    norm_gain,
    query_gain,
    key_norm_gain,
    key_matrix,
    value_matrix,
    lengths,
    owner,
):
    x, z, c = (lax.axis_index(a).astype(jnp.int32) for a in ("x", "z", "core"))
    zc = z * NC + c
    place = jnp.stack([x, z, c])
    fsdp = ("x", "z", "core")

    hidden = hidden_rows.astype(F32)
    mean_square = jnp.mean(hidden * hidden, axis=-1, keepdims=True)
    normed = (hidden * lax.rsqrt(mean_square + eps) * norm_gain).astype(BF)
    left = shift(normed, "x", NX, 1)
    right = shift(normed, "x", NX, -1)

    packed = jnp.concatenate(
        [key_matrix.reshape(SHARD, NX, 1, HEAD), value_matrix.reshape(SHARD, NX, 1, HEAD)], axis=2
    )
    packed = packed.transpose(1, 0, 2, 3).reshape(NX, SHARD, 2 * HEAD)
    piece = lax.all_to_all(packed, "x", split_axis=0, concat_axis=0, tiled=True)
    pieces = [piece]
    up = down = piece
    for _ in range(NZ // 2 - 1):
        up = shift(up, "z", NZ, 1)
        down = shift(down, "z", NZ, -1)
        pieces += [up, down]
    half = NX // 2
    pieces.append(
        jnp.concatenate(
            [shift(up[:half], "z", NZ, 1), shift(down[half:], "z", NZ, -1)], axis=0
        )
    )
    mine = jnp.stack(pieces)
    other = shift(mine, "core", NC, 1)

    far_a = shift(left[: ROWS // 2], "x", NX, 1)
    far_b = shift(right[ROWS // 2 :], "x", NX, -1)

    sent = queries.reshape(NZ * NC, RNG, NX, HEADS * HEAD).transpose(2, 0, 1, 3)
    sent = sent.reshape(NF, RNG, HEADS * HEAD)
    got = lax.all_to_all(sent, fsdp, split_axis=0, concat_axis=0, tiled=True)

    rows = jnp.arange(ROWS, dtype=jnp.int32)
    chunk_x = jnp.stack([(x + by + NX) % NX for by in X_ORDER])
    made = (rows[None, :] * NF + chunk_x[:, None] * (NZ * NC) + zc).reshape(-1)
    key_cos, key_sin = rope_tables(made - rollout_starts(lengths, owner, made))
    token = (
        (zc * RNG + jnp.arange(RNG, dtype=jnp.int32))[None, :] * NF
        + jnp.arange(NF, dtype=jnp.int32)[:, None]
    ).reshape(-1)
    start = rollout_starts(lengths, owner, token)
    q_cos, q_sin = rope_tables(token - start)
    key_rows = zc * RNG - HALO + jnp.arange(KROWS, dtype=jnp.int32)
    key_token = (
        key_rows[None, :, None] * NF
        + chunk_x[None, None, :] * (NZ * NC)
        + jnp.arange(NZ * NC, dtype=jnp.int32)[:, None, None]
    ).reshape(1, KTOK)

    ready = pl.pallas_call(
        prepare_kernel,
        grid=(HEADS,),
        in_specs=[
            pl.BlockSpec((QTOK, HEAD), lambda h: (0, h)),
            pl.BlockSpec((1, HEAD), lambda h: (0, 0)),
            pl.BlockSpec((QTOK, HEAD), lambda h: (0, 0)),
            pl.BlockSpec((QTOK, HEAD), lambda h: (0, 0)),
        ],
        out_specs=pl.BlockSpec((QTOK, HEAD), lambda h: (0, h)),
        out_shape=jax.ShapeDtypeStruct((QTOK, HEADS * HEAD), BF),
        name="prepare_queries",
    )(got.reshape(QTOK, HEADS * HEAD), query_gain.reshape(1, HEAD), q_cos, q_sin)

    vmem = pl.BlockSpec(memory_space=pltpu.VMEM)
    anywhere = pl.BlockSpec(memory_space=pl.ANY)
    made_kv = pl.pallas_call(
        project_kernel,
        in_specs=[pl.BlockSpec(memory_space=pltpu.SMEM)]
        + [vmem] * 5
        + [anywhere] * 2
        + [vmem] * 3,
        out_specs=vmem,
        out_shape=jax.ShapeDtypeStruct((NZ * NC, NX * KROWS, 2 * HEAD), BF),
        scratch_shapes=[
            pltpu.VMEM((NX, NZ, NC, SHARD, 2 * HEAD), BF),
            pltpu.VMEM((NX * ROWS, HEAD), F32),
            pltpu.VMEM((NX * ROWS, HEAD), F32),
            pltpu.SemaphoreType.DMA((2 * NZ,)),
        ],
        compiler_params=pltpu.CompilerParams(vmem_limit_bytes=40 * 2**20),
        name="project_keys_values",
    )(
        place,
        normed,
        left,
        right,
        far_a,
        far_b,
        mine,
        other,
        key_norm_gain.reshape(1, HEAD),
        key_cos,
        key_sin,
    )
    kv = lax.all_to_all(made_kv, ("z", "core"), split_axis=0, concat_axis=0, tiled=True)

    mixed = pl.pallas_call(
        attend_kernel,
        grid=(HEADS,),
        in_specs=[
            pl.BlockSpec((QTOK, HEAD), lambda h: (0, h)),
            pl.BlockSpec((KTOK, 2 * HEAD), lambda h: (0, 0)),
            pl.BlockSpec((QTOK, 1), lambda h: (0, 0)),
            pl.BlockSpec((QTOK, 1), lambda h: (0, 0)),
            pl.BlockSpec((1, KTOK), lambda h: (0, 0)),
        ],
        out_specs=pl.BlockSpec((QTOK, HEAD), lambda h: (0, h)),
        out_shape=jax.ShapeDtypeStruct((QTOK, HEADS * HEAD), BF),
        scratch_shapes=[
            pltpu.VMEM((QTOK, KTOK), F32),
            pltpu.VMEM((QTOK, KTOK), F32),
            pltpu.VMEM((QTOK, KTOK), BF),
        ],
        compiler_params=pltpu.CompilerParams(vmem_limit_bytes=32 * 2**20),
        name="attend",
    )(ready, kv.reshape(KTOK, 2 * HEAD), token[:, None], start[:, None], key_token)

    back = lax.all_to_all(
        mixed.reshape(NF, RNG, HEADS * HEAD), fsdp, split_axis=0, concat_axis=0, tiled=True
    )
    back = back.reshape(NX, NZ * NC, RNG, HEADS * HEAD).transpose(1, 2, 0, 3)
    return back.reshape(ROWS, NX * HEADS * HEAD)


def solution(mesh):
    grid = Mesh(mesh.devices.reshape(NX, NZ, NC, mesh.devices.shape[1]), ("x", "z", "core", "rep"))
    fsdp = ("x", "z", "core")
    whole = P(("rep",) + fsdp, None)
    placed = (whole, whole, P(), P(), P(), P(fsdp, None), P(fsdp, None), P("rep"), P("rep"))
    return jax.shard_map(
        per_device, mesh=grid, in_specs=placed, out_specs=whole, check_vma=False
    )
```

profile of v0, /device:TPU:1, one launch (start us, length us, event | category | flops | bytes accessed | tf_op | source)
XLA Modules:
  0.0 207.4 jit_solution(15756159801882968732)
XLA Ops:
  0.0 1.8 fusion
  1.8 0.0 copy-start.6
  1.8 0.0 copy-start.7
  1.8 1.1 fusion.2.own
  3.0 2.1 %collective-permute-start = (bf16[128,5120]{1,0:T(8,128)(2,1)S(1)}, bf16[128,5120]{1,0:T(8,128)(2,1)S(1)}, u32[]{:S(2)}, u32[]{:S(2)}) collective-permute-start(bf16[128,5120]{1,0:T(8,128)(2,1)S(1)} %fusion.2.own), channel_id=1, source_target_pairs={{0,64},{64,128},{128,192},{192,0},{1,65},{65,129},{129,193},{193,1... | collective-permute-start | bytes 3932168 | tf_op jit(solution)/shard_map/ppermute | solution.py:33
  5.1 1.4 collective-permute-start.1
  6.5 0.1 copy.21
  6.6 0.1 copy.22
  6.8 0.4 maximum_bitcast_fusion
  7.2 0.8 reshape.269
  7.9 3.5 %all-to-all-start.1 = ((bf16[4,80,256]{2,1,0:T(8,128)(2,1)}), bf16[4,80,256]{2,1,0:T(8,128)(2,1)S(1)}, u32[]{:S(2)}, u32[]{:S(2)}) async-start(bf16[4,80,256]{2,1,0:T(8,128)(2,1)} %reshape.269), calls=%async_computation.1 | async-start | bytes 327680 | tf_op jit(solution)/shard_map/all_to_all | solution.py:158
  11.5 2.3 %copy.20 = bf16[4,16,8,1024]{3,2,1,0:T(8,128)(2,1)} copy(bf16[4,16,8,1024]{3,2,0,1:T(8,128)(2,1)} %bitcast.50) | data formatting | bytes 2097152 | tf_op jit(solution)/shard_map/transpose | solution.py:177
  13.8 0.2 select_reduce_fusion.2
  14.0 23.2 %all-to-all-done.1 = bf16[4,80,256]{2,1,0:T(8,128)(2,1)S(1)} async-done(((bf16[4,80,256]{2,1,0:T(8,128)(2,1)}), bf16[4,80,256]{2,1,0:T(8,128)(2,1)S(1)}, u32[]{:S(2)}, u32[]{:S(2)}) %all-to-all-start.1) | async-done | bytes 163872 | tf_op jit(solution)/shard_map/all_to_all | solution.py:158
  37.2 12.5 %all-to-all-start = ((bf16[64,8,1024]{2,1,0:T(8,128)(2,1)}), bf16[64,8,1024]{2,1,0:T(8,128)(2,1)}, u32[]{:S(2)}, u32[]{:S(2)}) async-start(bf16[64,8,1024]{2,1,0:T(8,128)(2,1)} %bitcast.48), calls=%async_computation | async-start | bytes 2097152 | tf_op jit(solution)/shard_map/all_to_all | solution.py:179
  49.6 1.5 collective-permute-start.4
  51.1 1.3 collective-permute-start.5
  52.4 0.7 bitcast_dynamic-update-slice_fusion.6
  53.1 25.6 %collective-permute-done.4 = bf16[4,80,256]{2,1,0:T(8,128)(2,1)S(1)} collective-permute-done((bf16[4,80,256]{2,1,0:T(8,128)(2,1)S(1)}, bf16[4,80,256]{2,1,0:T(8,128)(2,1)S(1)}, u32[]{:S(2)}, u32[]{:S(2)}) %collective-permute-start.4) | collective-permute-done | bytes 163872 | tf_op jit(solution)/shard_map/ppermute | solution.py:33
  78.6 0.7 bitcast_dynamic-update-slice_fusion.5
  79.3 2.7 %collective-permute-start.7 = (bf16[4,80,256]{2,1,0:T(8,128)(2,1)S(1)}, bf16[4,80,256]{2,1,0:T(8,128)(2,1)S(1)}, u32[]{:S(2)}, u32[]{:S(2)}) collective-permute-start(bf16[4,80,256]{2,1,0:T(8,128)(2,1)S(1)} %collective-permute-done.5), channel_id=1, source_target_pairs={{0,56},{8,0},{16,8},{24,16},{32,24},{40,32},{48,40},{56,48},{1,57}... | collective-permute-start | bytes 491528 | tf_op jit(solution)/shard_map/ppermute | solution.py:33
  82.0 0.7 bitcast_dynamic-update-slice_fusion.4
  82.7 2.0 collective-permute-done.6
  84.7 0.7 bitcast_dynamic-update-slice_fusion.3
  85.4 2.7 %collective-permute-start.9 = (bf16[4,80,256]{2,1,0:T(8,128)(2,1)S(1)}, bf16[4,80,256]{2,1,0:T(8,128)(2,1)S(1)}, u32[]{:S(2)}, u32[]{:S(2)}) collective-permute-start(bf16[4,80,256]{2,1,0:T(8,128)(2,1)S(1)} %collective-permute-done.7), channel_id=1, source_target_pairs={{0,56},{8,0},{16,8},{24,16},{32,24},{40,32},{48,40},{56,48},{1,57}... | collective-permute-start | bytes 491528 | tf_op jit(solution)/shard_map/ppermute | solution.py:33
  88.1 0.7 bitcast_dynamic-update-slice_fusion.2
  88.7 1.3 collective-permute-done.8
  90.1 0.2 collective-permute-done.9
  90.3 3.1 %collective-permute-start.11 = (bf16[2,80,256]{2,1,0:T(8,128)(2,1)S(1)}, bf16[2,80,256]{2,1,0:T(8,128)(2,1)S(1)}, u32[]{:S(2)}, u32[]{:S(2)}) collective-permute-start(bf16[2,80,256]{2,1,0:T(8,128)(2,1)S(1)} %slice.19), channel_id=1, source_target_pairs={{0,56},{8,0},{16,8},{24,16},{32,24},{40,32},{48,40},{56,48},{1,57}... | collective-permute-start | bytes 245768 | tf_op jit(solution)/shard_map/ppermute | solution.py:33
  93.5 0.7 bitcast_dynamic-update-slice_fusion.1
  94.1 0.7 bitcast_dynamic-update-slice_fusion
  94.8 0.1 collective-permute-done.11
  94.9 0.7 fusion.3.mine
  95.6 4.1 %collective-permute-start.12 = (bf16[8,4,80,256]{3,2,1,0:T(8,128)(2,1)}, bf16[8,4,80,256]{3,2,1,0:T(8,128)(2,1)}, u32[]{:S(2)}, u32[]{:S(2)}) collective-permute-start(bf16[8,4,80,256]{3,2,1,0:T(8,128)(2,1)} %fusion.3.mine), channel_id=1, source_target_pairs={{0,4},{4,0},{1,5},{5,1},{2,6},{6,2},{3,7},{7,3},{8,12},{12,8},{9,1... | collective-permute-start | bytes 3932168 | tf_op jit(solution)/shard_map/ppermute | solution.py:33
  99.7 0.1 add_multiply_fusion
  99.7 0.1 add.186
  99.8 0.1 add_bitcast_fusion
  99.9 0.1 select_reduce_fusion
  100.0 0.1 subtract_convert_fusion
  100.1 0.9 slice.16
  101.0 1.3 collective-permute-start.2
  102.3 2.0 slice.17
  104.3 1.4 collective-permute-start.3
  105.7 0.6 negate_power_fusion
  106.3 0.1 pad_add_fusion.place
  106.3 3.3 %fusion.5 = (f32[512,64]{1,0:T(8,128)S(1)}, f32[512,64]{1,0:T(8,128)S(1)}, f32[512,64]{1,0:T(8,128)S(1)}, f32[512,64]{1,0:T(8,128)}, f32[512,64]{1,0:T(8,128)S(1)}, /*index=5*/f32[512,64]{1,0:T(8,128)}) fusion(f32[64]{0:T(128)} %negate_power_fusion, f32[512]{0:T(512)S(1)} %get-tuple-element.16, f32[512]{0:T(512)S(1)} %get-tuple-element.17), kind=kLoop, calls=%fused_computation.27 | loop fusion | flops 131072 | bytes 790784 | tf_op jit(solution)/shard_map/neg | solution.py:54
  109.6 0.1 pad_maximum_fusion.2.cosine
  109.8 0.1 pad_maximum_fusion.3.sine
  109.9 8.9 %collective-permute-done.2.far_a = bf16[64,5120]{1,0:T(8,128)(2,1)S(1)} collective-permute-done((bf16[64,5120]{1,0:T(8,128)(2,1)}, bf16[64,5120]{1,0:T(8,128)(2,1)S(1)}, u32[]{:S(2)}, u32[]{:S(2)}) %collective-permute-start.2) | collective-permute-done | bytes 655392 | tf_op jit(solution)/shard_map/ppermute | solution.py:33
  118.8 1.8 collective-permute-done.3.far_b
  120.6 5.9 %project_keys_values.1 = bf16[16,48,256]{2,1,0:T(8,128)(2,1)} custom-call(s32[3]{0:T(128)S(1)} %pad_add_fusion.place, bf16[128,5120]{1,0:T(8,128)(2,1)S(1)} %fusion.2.own, bf16[128,5120]{1,0:T(8,128)(2,1)S(1)} %collective-permute-done.left, bf16[128,5120]{1,0:T(8,128)(2,1)} %collective-permute-done.1.right, ...), custom_call_target="tpu_custom_call" | custom-call | tf_op jit(solution)/shard_map/project_keys_values/pallas_call | solution.py:214
  126.6 6.9 %all-to-all-start.2 = ((bf16[16,48,256]{2,1,0:T(8,128)(2,1)}), bf16[16,48,256]{2,1,0:T(8,128)(2,1)S(1)}, u32[]{:S(2)}, u32[]{:S(2)}) async-start(bf16[16,48,256]{2,1,0:T(8,128)(2,1)} %project_keys_values.1), calls=%async_computation.2 | async-start | bytes 786432 | tf_op jit(solution)/shard_map/all_to_all | solution.py:243
  133.5 0.9 add.213.token
  134.4 0.1 copy.24.start
  134.5 0.1 broadcast_add_fusion
  134.6 0.1 add.212.key_token
  134.7 0.8 pad_maximum_fusion.cosine
  135.6 0.8 pad_maximum_fusion.1.sine
  136.4 6.2 %prepare_queries.1.q = bf16[512,1024]{1,0:T(8,128)(2,1)} custom-call(bf16[512,1024]{1,0:T(8,128)(2,1)} %bitcast.3.q, f32[1,128]{1,0:T(1,128)} %bitcast.52, f32[512,128]{1,0:T(8,128)} %pad_maximum_fusion.cosine, f32[512,128]{1,0:T(8,128)} %pad_maximum_fusion.1.sine), custom_call_target="tpu_custom_call" | custom-call | tf_op jit(solution)/shard_map/prepare_queries/pallas_call | solution.py:198
  142.6 5.4 %all-to-all-done.2 = bf16[16,48,256]{2,1,0:T(8,128)(2,1)S(1)} async-done(((bf16[16,48,256]{2,1,0:T(8,128)(2,1)}), bf16[16,48,256]{2,1,0:T(8,128)(2,1)S(1)}, u32[]{:S(2)}, u32[]{:S(2)}) %all-to-all-start.2) | async-done | bytes 393248 | tf_op jit(solution)/shard_map/all_to_all | solution.py:243
  148.0 1.2 copy-done
  149.3 23.0 %attend.1 = bf16[512,1024]{1,0:T(8,128)(2,1)S(1)} custom-call(bf16[512,1024]{1,0:T(8,128)(2,1)S(1)} %copy-done, bf16[768,256]{1,0:T(8,128)(2,1)S(1)} %bitcast.46, s32[512,1]{1,0:T(8,128)S(1)} %add.213.token, s32[512,1]{1,0:T(8,128)S(1)} %copy.24.start, s32[1,768]{1,0:T(1,128)S(1)} %add.212.key_token), custom_call_target="tpu_custom_call" | custom-call | tf_op jit(solution)/shard_map/attend/pallas_call | solution.py:245
  172.3 34.1 %all_to_all.20 = bf16[64,8,1024]{2,1,0:T(8,128)(2,1)S(1)} all-to-all(bf16[64,8,1024]{2,1,0:T(8,128)(2,1)S(1)} %bitcast.45), channel_id=1, replica_groups=mesh['x'=4,'z'=8,'core'=2,'rep'=4] {'x','z','core'}, dimensions={0} | all-to-all | bytes 2097152 | tf_op jit(solution)/shard_map/all_to_all | solution.py:266
  206.4 1.1 copy.25
  (37 shorter events, 0.2 us)
Async XLA Ops:
  0.0 1.8 copy-start.2
  1.8 4.7 %copy-start.6 = (bf16[80,512]{1,0:T(8,128)(2,1)S(1)}, bf16[80,512]{1,0:T(8,128)(2,1)}, u32[]{:S(2)}) copy-start(bf16[80,512]{1,0:T(8,128)(2,1)} %param.14) | copy-start | bytes 245764
  1.8 4.8 %copy-start.7 = (bf16[80,512]{1,0:T(8,128)(2,1)S(1)}, bf16[80,512]{1,0:T(8,128)(2,1)}, u32[]{:S(2)}) copy-start(bf16[80,512]{1,0:T(8,128)(2,1)} %param.15) | copy-start | bytes 245764
  3.0 97.2 %collective-permute-start = (bf16[128,5120]{1,0:T(8,128)(2,1)S(1)}, bf16[128,5120]{1,0:T(8,128)(2,1)S(1)}, u32[]{:S(2)}, u32[]{:S(2)}) collective-permute-start(bf16[128,5120]{1,0:T(8,128)(2,1)S(1)} %fusion.2.own), channel_id=1, source_target_pairs={{0,64},{64,128},{128,192},{192,0},{1,65},{65,129},{129,193},{193,1... | collective-permute-start | bytes 3932168 | tf_op jit(solution)/shard_map/ppermute | solution.py:33
  5.1 97.2 %collective-permute-start.1 = (bf16[128,5120]{1,0:T(8,128)(2,1)S(1)}, bf16[128,5120]{1,0:T(8,128)(2,1)}, u32[]{:S(2)}, u32[]{:S(2)}) collective-permute-start(bf16[128,5120]{1,0:T(8,128)(2,1)S(1)} %fusion.2.own), channel_id=1, source_target_pairs={{0,192},{64,0},{128,64},{192,128},{1,193},{65,1},{129,65},{193,129... | collective-permute-start | bytes 3932168 | tf_op jit(solution)/shard_map/ppermute | solution.py:33
  7.9 5.9 %copy-start.8 = (s32[64]{0:T(128)S(1)}, s32[64]{0:T(128)}, u32[]{:S(2)}) copy-start(s32[64]{0:T(128)} %param.17) | copy-start | bytes 772
  7.9 5.9 %copy-start.9 = (s32[64]{0:T(128)S(1)}, s32[64]{0:T(128)}, u32[]{:S(2)}) copy-start(s32[64]{0:T(128)} %param.16) | copy-start | bytes 772
  7.9 29.2 %all-to-all-start.1 = ((bf16[4,80,256]{2,1,0:T(8,128)(2,1)}), bf16[4,80,256]{2,1,0:T(8,128)(2,1)S(1)}, u32[]{:S(2)}, u32[]{:S(2)}) async-start(bf16[4,80,256]{2,1,0:T(8,128)(2,1)} %reshape.269), calls=%async_computation.1 | async-start | bytes 327680 | tf_op jit(solution)/shard_map/all_to_all | solution.py:158
  11.5 88.3 %copy-start.5 = (s32[64,8]{1,0:T(8,128)}, s32[64,8]{1,0:T(8,128)S(1)}, u32[]{:S(2)}) copy-start(s32[64,8]{1,0:T(8,128)S(1)} %iota_add_fusion.1) | copy-start | bytes 6148
  37.2 89.4 %all-to-all-start = ((bf16[64,8,1024]{2,1,0:T(8,128)(2,1)}), bf16[64,8,1024]{2,1,0:T(8,128)(2,1)}, u32[]{:S(2)}, u32[]{:S(2)}) async-start(bf16[64,8,1024]{2,1,0:T(8,128)(2,1)} %bitcast.48), calls=%async_computation | async-start | bytes 2097152 | tf_op jit(solution)/shard_map/all_to_all | solution.py:179
  49.6 29.0 %collective-permute-start.4 = (bf16[4,80,256]{2,1,0:T(8,128)(2,1)S(1)}, bf16[4,80,256]{2,1,0:T(8,128)(2,1)S(1)}, u32[]{:S(2)}, u32[]{:S(2)}) collective-permute-start(bf16[4,80,256]{2,1,0:T(8,128)(2,1)S(1)} %all-to-all-done.1), channel_id=1, source_target_pairs={{0,8},{8,16},{16,24},{24,32},{32,40},{40,48},{48,56},{56,0},{1,9},... | collective-permute-start | bytes 491528 | tf_op jit(solution)/shard_map/ppermute | solution.py:33
  51.1 28.2 %collective-permute-start.5 = (bf16[4,80,256]{2,1,0:T(8,128)(2,1)S(1)}, bf16[4,80,256]{2,1,0:T(8,128)(2,1)S(1)}, u32[]{:S(2)}, u32[]{:S(2)}) collective-permute-start(bf16[4,80,256]{2,1,0:T(8,128)(2,1)S(1)} %all-to-all-done.1), channel_id=1, source_target_pairs={{0,56},{8,0},{16,8},{24,16},{32,24},{40,32},{48,40},{56,48},{1,57}... | collective-permute-start | bytes 491528 | tf_op jit(solution)/shard_map/ppermute | solution.py:33
  78.6 6.1 %collective-permute-start.6 = (bf16[4,80,256]{2,1,0:T(8,128)(2,1)S(1)}, bf16[4,80,256]{2,1,0:T(8,128)(2,1)S(1)}, u32[]{:S(2)}, u32[]{:S(2)}) collective-permute-start(bf16[4,80,256]{2,1,0:T(8,128)(2,1)S(1)} %collective-permute-done.4), channel_id=1, source_target_pairs={{0,8},{8,16},{16,24},{24,32},{32,40},{40,48},{48,56},{56,0},{1,9},... | collective-permute-start | bytes 491528 | tf_op jit(solution)/shard_map/ppermute | solution.py:33
  79.3 6.1 %collective-permute-start.7 = (bf16[4,80,256]{2,1,0:T(8,128)(2,1)S(1)}, bf16[4,80,256]{2,1,0:T(8,128)(2,1)S(1)}, u32[]{:S(2)}, u32[]{:S(2)}) collective-permute-start(bf16[4,80,256]{2,1,0:T(8,128)(2,1)S(1)} %collective-permute-done.5), channel_id=1, source_target_pairs={{0,56},{8,0},{16,8},{24,16},{32,24},{40,32},{48,40},{56,48},{1,57}... | collective-permute-start | bytes 491528 | tf_op jit(solution)/shard_map/ppermute | solution.py:33
  84.7 5.4 %collective-permute-start.8 = (bf16[4,80,256]{2,1,0:T(8,128)(2,1)S(1)}, bf16[4,80,256]{2,1,0:T(8,128)(2,1)S(1)}, u32[]{:S(2)}, u32[]{:S(2)}) collective-permute-start(bf16[4,80,256]{2,1,0:T(8,128)(2,1)S(1)} %collective-permute-done.6), channel_id=1, source_target_pairs={{0,8},{8,16},{16,24},{24,32},{32,40},{40,48},{48,56},{56,0},{1,9},... | collective-permute-start | bytes 491528 | tf_op jit(solution)/shard_map/ppermute | solution.py:33
  85.4 4.9 %collective-permute-start.9 = (bf16[4,80,256]{2,1,0:T(8,128)(2,1)S(1)}, bf16[4,80,256]{2,1,0:T(8,128)(2,1)S(1)}, u32[]{:S(2)}, u32[]{:S(2)}) collective-permute-start(bf16[4,80,256]{2,1,0:T(8,128)(2,1)S(1)} %collective-permute-done.7), channel_id=1, source_target_pairs={{0,56},{8,0},{16,8},{24,16},{32,24},{40,32},{48,40},{56,48},{1,57}... | collective-permute-start | bytes 491528 | tf_op jit(solution)/shard_map/ppermute | solution.py:33
  90.1 4.7 %collective-permute-start.10 = (bf16[2,80,256]{2,1,0:T(8,128)(2,1)S(1)}, bf16[2,80,256]{2,1,0:T(8,128)(2,1)S(1)}, u32[]{:S(2)}, u32[]{:S(2)}) collective-permute-start(bf16[2,80,256]{2,1,0:T(8,128)(2,1)S(1)} %slice.18), channel_id=1, source_target_pairs={{0,8},{8,16},{16,24},{24,32},{32,40},{40,48},{48,56},{56,0},{1,9},... | collective-permute-start | bytes 245768 | tf_op jit(solution)/shard_map/ppermute | solution.py:33
  90.3 4.6 %collective-permute-start.11 = (bf16[2,80,256]{2,1,0:T(8,128)(2,1)S(1)}, bf16[2,80,256]{2,1,0:T(8,128)(2,1)S(1)}, u32[]{:S(2)}, u32[]{:S(2)}) collective-permute-start(bf16[2,80,256]{2,1,0:T(8,128)(2,1)S(1)} %slice.19), channel_id=1, source_target_pairs={{0,56},{8,0},{16,8},{24,16},{32,24},{40,32},{48,40},{56,48},{1,57}... | collective-permute-start | bytes 245768 | tf_op jit(solution)/shard_map/ppermute | solution.py:33
  95.6 25.0 %collective-permute-start.12 = (bf16[8,4,80,256]{3,2,1,0:T(8,128)(2,1)}, bf16[8,4,80,256]{3,2,1,0:T(8,128)(2,1)}, u32[]{:S(2)}, u32[]{:S(2)}) collective-permute-start(bf16[8,4,80,256]{3,2,1,0:T(8,128)(2,1)} %fusion.3.mine), channel_id=1, source_target_pairs={{0,4},{4,0},{1,5},{5,1},{2,6},{6,2},{3,7},{7,3},{8,12},{12,8},{9,1... | collective-permute-start | bytes 3932168 | tf_op jit(solution)/shard_map/ppermute | solution.py:33
  101.0 17.8 %collective-permute-start.2 = (bf16[64,5120]{1,0:T(8,128)(2,1)}, bf16[64,5120]{1,0:T(8,128)(2,1)S(1)}, u32[]{:S(2)}, u32[]{:S(2)}) collective-permute-start(bf16[64,5120]{1,0:T(8,128)(2,1)} %slice.16), channel_id=1, source_target_pairs={{0,64},{64,128},{128,192},{192,0},{1,65},{65,129},{129,193},{193,1... | collective-permute-start | bytes 1966088 | tf_op jit(solution)/shard_map/ppermute | solution.py:33
  104.3 16.4 %collective-permute-start.3 = (bf16[64,5120]{1,0:T(8,128)(2,1)}, bf16[64,5120]{1,0:T(8,128)(2,1)}, u32[]{:S(2)}, u32[]{:S(2)}) collective-permute-start(bf16[64,5120]{1,0:T(8,128)(2,1)} %slice.17), channel_id=1, source_target_pairs={{0,192},{64,0},{128,64},{192,128},{1,193},{65,1},{129,65},{193,129... | collective-permute-start | bytes 1966088 | tf_op jit(solution)/shard_map/ppermute | solution.py:33
  106.3 14.3 %copy-start.1 = (f32[128]{0:T(128)S(1)}, f32[128]{0:T(128)}, u32[]{:S(2)}) copy-start(f32[128]{0:T(128)} %param.13) | copy-start | bytes 1540
  126.5 8.2 %copy-start.4 = (f32[512,64]{1,0:T(8,128)S(1)}, f32[512,64]{1,0:T(8,128)}, u32[]{:S(2)}) copy-start(f32[512,64]{1,0:T(8,128)} %get-tuple-element.13) | copy-start | bytes 393220
  126.6 9.0 %copy-start.3 = (f32[512,64]{1,0:T(8,128)S(1)}, f32[512,64]{1,0:T(8,128)}, u32[]{:S(2)}) copy-start(f32[512,64]{1,0:T(8,128)} %get-tuple-element.15) | copy-start | bytes 393220
  126.6 21.5 %all-to-all-start.2 = ((bf16[16,48,256]{2,1,0:T(8,128)(2,1)}), bf16[16,48,256]{2,1,0:T(8,128)(2,1)S(1)}, u32[]{:S(2)}, u32[]{:S(2)}) async-start(bf16[16,48,256]{2,1,0:T(8,128)(2,1)} %project_keys_values.1), calls=%async_computation.2 | async-start | bytes 786432 | tf_op jit(solution)/shard_map/all_to_all | solution.py:243
  148.0 1.2 copy-start
where the time goes:
time: 208 us; the launch traced here: 207 us
  waiting for transfers between devices  68.6 us (33%)
  starting transfers between devices  44.3 us (21%)
  Pallas kernels  35.1 us (17%)
  blocking collectives  34.1 us (16%)
  local copies, waits for them, and re-layouts  14.6 us (7%)
  other arithmetic  10.4 us (5%)
    ppermute x13, waiting for transfers between devices, shift(): lax.ppermute(value, axis, [(i, (i + by) % size) for i in range(size)])  40 us
    all_to_all x1, blocking collectives, per_device(): lax.all_to_all(mixed.reshape(NF, RNG, HEADS * HEAD), fsdp, split_axis=0,...  34.1 us
    all_to_all x1, waiting for transfers between devices, per_device(): piece = lax.all_to_all(packed, 'x', split_axis=0, concat_axis=0, tiled=True)  23.2 us
    pallas_call x1, Pallas kernels, per_device(): pl.pallas_call(attend_kernel, grid=(HEADS,), in_specs=[pl.BlockSpec((QTOK...  23 us
    ppermute x13, starting transfers between devices, shift(): lax.ppermute(value, axis, [(i, (i + by) % size) for i in range(size)])  21.5 us
    all_to_all x1, starting transfers between devices, per_device(): got = lax.all_to_all(sent, fsdp, split_axis=0, concat_axis=0, tiled=True)  12.5 us
    all_to_all x1, starting transfers between devices, per_device(): lax.all_to_all(made_kv, ('z', 'core'), split_axis=0, concat_axis=0, tiled...  6.91 us
    pallas_call x1, Pallas kernels, per_device(): pl.pallas_call(prepare_kernel, grid=(HEADS,), in_specs=[pl.BlockSpec((QTO...  6.21 us
  transfers between devices with their start and end apart: 16, of which 9 were waited for; matrix products, arithmetic and copies ran while one was open for 10% of the time, Pallas kernels for 6%

commit v1 on v0

v1 whole, which is shorter than its diff:
```python
import functools

import jax
import jax.numpy as jnp
import numpy as np
from jax import lax
from jax.experimental import pallas as pl
from jax.experimental.pallas import tpu as pltpu
from jax.sharding import Mesh, PartitionSpec as P

NX, NZ, NC = 4, 8, 2
NF = NX * NZ * NC
WIDTH = 5120
HEADS = 8
HEAD = 128
ROWS = 128
SHARD = WIDTH // NF
RNG = 8
HALO = 4
KROWS = RNG + HALO
QTOK = NF * RNG
KTOK = NF * KROWS
PAIR = 2 * NF
WINDOW = (HALO + 2) * NF
X_ORDER = (0, -1, 1, 2)
Z_ORDER = (0, -1, 1, -2, 2, -3, 3, 4)
NEAR = 5

eps = 1e-06
rope_base = 1000000.0
BF = jnp.bfloat16
F32 = jnp.float32


def shift(value, axis, size, by):
    return lax.ppermute(value, axis, [(i, (i + by) % size) for i in range(size)])


def rollout_starts(lengths, owner, tokens):
    index = jnp.arange(lengths.shape[0], dtype=jnp.int32)
    earlier = (owner[None, :] < owner[:, None]) | (owner[None, :] == owner[:, None]) & (
        index[None, :] < index[:, None]
    )
    offset = jnp.sum(jnp.where(earlier, lengths[None, :], 0), axis=1)
    return jnp.max(jnp.where(offset[None, :] <= tokens[:, None], offset[None, :], 0), axis=1)


def rope_tables(positions):
    half = HEAD // 2
    steps = jnp.arange(half, dtype=F32) * (2.0 / HEAD)
    inverse = jnp.power(F32(rope_base), -steps)
    angles = positions.astype(F32)[:, None] * inverse[None, :]
    cosine = jnp.cos(angles)
    sine = jnp.sin(angles)
    return (
        jnp.concatenate([cosine, cosine], axis=1),
        jnp.concatenate([-sine, sine], axis=1),
    )


def normed_rope(value, gain, cosine, sine):
    mean_square = jnp.mean(value * value, axis=-1, keepdims=True)
    value = value * lax.rsqrt(mean_square + eps) * gain
    return value * cosine + pltpu.roll(value, HEAD // 2, 1) * sine


def pack_kernel(place, key, value, *out):
    for k, by in enumerate(X_ORDER):
        head = lax.rem(place[0] - by + NX, NX)
        lanes = pl.ds(pl.multiple_of(head * HEAD, HEAD), HEAD)
        out[k][:, :HEAD] = key[:, lanes]
        out[k][:, HEAD:] = value[:, lanes]


def norm_kernel(hidden, gain, top, low):
    block = 16
    for out, base in ((top, 0), (low, ROWS // 2)):
        for i in range(0, ROWS // 2, block):
            value = hidden[base + i : base + i + block, :].astype(F32)
            mean_square = jnp.mean(value * value, axis=-1, keepdims=True)
            value = value * lax.rsqrt(mean_square + eps) * gain[...]
            out[i : i + block, :] = value.astype(BF)


def project(x, w, gain, cosine, sine):
    raw = jnp.dot(x, w, preferred_element_type=F32)
    return normed_rope(raw[:, :HEAD], gain, cosine, sine), raw[:, HEAD:]


def first_kernel(
    place,
    own_a,
    own_b,
    left_a,
    left_b,
    right_a,
    right_b,
    mine,
    mine2,
    other,
    other2,
    gain,
    cosine,
    sine,
    out,
    weight,
    sem,
):
    x, z, c = place[0], place[1], place[2]
    copies = []
    for k, by in enumerate(Z_ORDER):
        at = lax.rem(z + by + NZ, NZ)
        near = k < NEAR
        for which, core in (((mine, mine2)[k >= NEAR], c), ((other, other2)[k >= NEAR], 1 - c)):
            for i, step in enumerate(X_ORDER):
                copies.append(
                    pltpu.make_async_copy(
                        which.at[k if near else k - NEAR, i],
                        weight.at[lax.rem(x + step + NX, NX), at, core],
                        sem.at[len(copies)],
                    )
                )
    for copy in copies:
        copy.start()
    for copy in copies:
        copy.wait()
    w = weight[...].reshape(WIDTH, 2 * HEAD)
    for k in range(NX - 1):
        top, low = ((own_a, own_b), (left_a, left_b), (right_a, right_b))[k]
        tokens = jnp.concatenate([top[...], low[...]], axis=0)
        rows = pl.ds(k * ROWS, ROWS)
        key, value = project(tokens, w, gain[...], cosine[rows, :], sine[rows, :])
        out[k, 0] = key
        out[k, 1] = value


def second_kernel(far_a, far_b, weight, made, gain, cosine, sine, out, keep_k, keep_v):
    w = weight[...].reshape(WIDTH, 2 * HEAD)
    x = jnp.concatenate([far_a[...], far_b[...]], axis=0)
    rows = pl.ds((NX - 1) * ROWS, ROWS)
    far = project(x, w, gain[...], cosine[rows, :], sine[rows, :])
    for side, (keep, lanes) in enumerate(((keep_k, pl.ds(0, HEAD)), (keep_v, pl.ds(HEAD, HEAD)))):
        for k in range(NX - 1):
            keep[pl.ds(k, ROWS, stride=NX), :] = made[k, side]
        keep[pl.ds(NX - 1, ROWS, stride=NX), :] = far[side]
        out[0, : NX * HALO, lanes] = jnp.zeros((NX * HALO, HEAD), BF)
        out[0, NX * HALO :, lanes] = keep[: NX * RNG, :].astype(BF)
        for j in range(1, NZ * NC):
            start = NX * (RNG * j - HALO)
            out[j, :, lanes] = keep[start : start + NX * KROWS, :].astype(BF)


def prepare_kernel(q, gain, cosine, sine, out, wide):
    for h in range(HEADS):
        wide[h] = q[:, pl.ds(h * HEAD, HEAD)].astype(F32)
    for r in range(RNG):
        rows = pl.ds(r * NF, NF)
        for h in range(HEADS):
            value = wide[h, pl.ds(r, NF, stride=RNG), :]
            value = normed_rope(value, gain[...], cosine[rows, :], sine[rows, :])
            out[r // 2, pl.ds(h * PAIR + (r % 2) * NF, NF), :] = value.astype(BF)


def attend_kernel(q, kv, token, start, key_token, out, bias, kept, mixed, probs, scores):
    wide = kv[...].astype(F32)
    for i in range(KROWS // 2):
        part = wide[:, 2 * NX * i : 2 * NX * (i + 1), :].reshape(PAIR, 2 * HEAD)
        kept[pl.ds(i * PAIR, PAIR), :] = part.astype(BF)
    scale = np.float32(1.0 / np.sqrt(HEAD))
    for i in range(RNG // 2):
        rows = pl.ds(i * PAIR, PAIR)
        window = pl.ds(i * PAIR, WINDOW)
        key = key_token[:, i * PAIR : i * PAIR + WINDOW]
        seen = (key >= start[rows, :]) & (key <= token[rows, :])
        bias[...] = jnp.where(seen, 0.0, -jnp.inf)
        scores[...] = lax.dot_general(
            q[i], kept[window, :HEAD], (((1,), (1,)), ((), ())), preferred_element_type=F32
        )
        for h in range(HEADS):
            head = pl.ds(h * PAIR, PAIR)
            s = scores[head, :] * scale + bias[...]
            weights = jnp.exp(s - jnp.max(s, axis=1, keepdims=True))
            total = jnp.sum(weights, axis=1, keepdims=True)
            probs[head, :] = (weights * (1.0 / total)).astype(BF)
        m = jnp.dot(probs[...], kept[window, HEAD:], preferred_element_type=F32)
        for h in range(HEADS):
            for r in range(2):
                mixed[h, pl.ds(2 * i + r, NF, stride=RNG), :] = m[h * PAIR + r * NF :][:NF]
    for h in range(HEADS):
        out[:, pl.ds(h * HEAD, HEAD)] = mixed[h].astype(BF)


def per_device(
    hidden_rows,
    queries,
    norm_gain,
    query_gain,
    key_norm_gain,
    key_matrix,
    value_matrix,
    lengths,
    owner,
):
    x, z, c = (lax.axis_index(a).astype(jnp.int32) for a in ("x", "z", "core"))
    zc = z * NC + c
    place = jnp.stack([x, z, c])
    fsdp = ("x", "z", "core")

    vmem = pl.BlockSpec(memory_space=pltpu.VMEM)
    smem = pl.BlockSpec(memory_space=pltpu.SMEM)
    packed = pl.pallas_call(
        pack_kernel,
        in_specs=[smem, vmem, vmem],
        out_specs=[vmem] * NX,
        out_shape=[jax.ShapeDtypeStruct((SHARD, 2 * HEAD), BF)] * NX,
        name="pack_weights",
    )(place, key_matrix, value_matrix)
    piece = jnp.stack(
        [packed[0]] + [shift(packed[k], "x", NX, -X_ORDER[k]) for k in range(1, NX)]
    )

    cut = ROWS // 2
    own_a, own_b = pl.pallas_call(
        norm_kernel,
        in_specs=[vmem, vmem],
        out_specs=[vmem] * 2,
        out_shape=[jax.ShapeDtypeStruct((cut, WIDTH), BF)] * 2,
        name="norm_hidden",
    )(hidden_rows, norm_gain.reshape(1, WIDTH))
    left_a = shift(own_a, "x", NX, 1)
    right_b = shift(own_b, "x", NX, -1)
    left_b = shift(own_b, "x", NX, 1)
    right_a = shift(own_a, "x", NX, -1)

    pieces = [piece]
    up = down = piece
    for step in range(NZ // 2 - 1):
        up = shift(up, "z", NZ, 1)
        down = shift(down, "z", NZ, -1)
        if step == 0:
            up, down, left_a, right_b = lax.optimization_barrier((up, down, left_a, right_b))
            far_a = shift(left_a, "x", NX, 1)
            far_b = shift(right_b, "x", NX, -1)
        pieces += [up, down]
    half = NX // 2
    last_a = shift(up[:half], "z", NZ, 1)
    last_b = shift(down[half:], "z", NZ, -1)
    pieces.append(jnp.concatenate([last_a, last_b], axis=0))
    mine, mine2 = jnp.stack(pieces[:NEAR]), jnp.stack(pieces[NEAR:])
    other, other2 = shift(mine, "core", NC, 1), shift(mine2, "core", NC, 1)

    sent = queries.reshape(NZ * NC, RNG, NX, HEADS * HEAD).transpose(2, 0, 1, 3)
    sent = sent.reshape(NF, RNG, HEADS * HEAD)
    got = lax.all_to_all(sent, fsdp, split_axis=0, concat_axis=0, tiled=True)

    rows = jnp.arange(ROWS, dtype=jnp.int32)
    chunk_x = jnp.stack([(x + by + NX) % NX for by in X_ORDER])
    made = (rows[None, :] * NF + chunk_x[:, None] * (NZ * NC) + zc).reshape(-1)
    key_cos, key_sin = rope_tables(made - rollout_starts(lengths, owner, made))
    token = zc * QTOK + jnp.arange(QTOK, dtype=jnp.int32)
    start = rollout_starts(lengths, owner, token)
    q_cos, q_sin = rope_tables(token - start)
    pair_rows = zc * RNG - HALO + jnp.arange(KROWS, dtype=jnp.int32).reshape(KROWS // 2, 1, 2, 1)
    key_token = (
        pair_rows * NF
        + chunk_x[None, None, None, :] * (NZ * NC)
        + jnp.arange(NZ * NC, dtype=jnp.int32)[None, :, None, None]
    ).reshape(1, KTOK)

    ready = pl.pallas_call(
        prepare_kernel,
        in_specs=[vmem] * 4,
        out_specs=vmem,
        out_shape=jax.ShapeDtypeStruct((RNG // 2, HEADS * PAIR, HEAD), BF),
        scratch_shapes=[pltpu.VMEM((HEADS, QTOK, HEAD), F32)],
        compiler_params=pltpu.CompilerParams(vmem_limit_bytes=32 * 2**20),
        name="prepare_queries",
    )(got.reshape(QTOK, HEADS * HEAD), query_gain.reshape(1, HEAD), q_cos, q_sin)

    anywhere = pl.BlockSpec(memory_space=pl.ANY)
    key_gain = key_norm_gain.reshape(1, HEAD)
    made_first, weight = pl.pallas_call(
        first_kernel,
        in_specs=[smem]
        + [vmem] * 6
        + [anywhere] * 4
        + [vmem] * 3,
        out_specs=[vmem] * 2,
        out_shape=[
            jax.ShapeDtypeStruct((NX - 1, 2, ROWS, HEAD), F32),
            jax.ShapeDtypeStruct((NX, NZ, NC, SHARD, 2 * HEAD), BF),
        ],
        scratch_shapes=[pltpu.SemaphoreType.DMA((2 * NZ * NX,))],
        compiler_params=pltpu.CompilerParams(vmem_limit_bytes=32 * 2**20),
        name="project_first",
    )(
        place,
        own_a,
        own_b,
        left_a,
        left_b,
        right_a,
        right_b,
        mine,
        mine2,
        other,
        other2,
        key_gain,
        key_cos,
        key_sin,
    )
    made_kv = pl.pallas_call(
        second_kernel,
        in_specs=[vmem] * 7,
        out_specs=vmem,
        out_shape=jax.ShapeDtypeStruct((NZ * NC, NX * KROWS, 2 * HEAD), BF),
        scratch_shapes=[pltpu.VMEM((NX * ROWS, HEAD), F32)] * 2,
        compiler_params=pltpu.CompilerParams(vmem_limit_bytes=32 * 2**20),
        name="project_last",
    )(far_a, far_b, weight, made_first, key_gain, key_cos, key_sin)
    kv = lax.all_to_all(made_kv, ("z", "core"), split_axis=0, concat_axis=0, tiled=True)

    mixed = pl.pallas_call(
        attend_kernel,
        in_specs=[vmem] * 5,
        out_specs=vmem,
        out_shape=jax.ShapeDtypeStruct((QTOK, HEADS * HEAD), BF),
        scratch_shapes=[
            pltpu.VMEM((PAIR, WINDOW), F32),
            pltpu.VMEM((KTOK, 2 * HEAD), BF),
            pltpu.VMEM((HEADS, QTOK, HEAD), F32),
            pltpu.VMEM((HEADS * PAIR, WINDOW), BF),
            pltpu.VMEM((HEADS * PAIR, WINDOW), F32),
        ],
        compiler_params=pltpu.CompilerParams(vmem_limit_bytes=32 * 2**20),
        name="attend",
    )(ready, kv, token[:, None], start[:, None], key_token)

    back = lax.all_to_all(
        mixed.reshape(NF, RNG, HEADS * HEAD), fsdp, split_axis=0, concat_axis=0, tiled=True
    )
    back = back.reshape(NX, NZ * NC, RNG, HEADS * HEAD).transpose(1, 2, 0, 3)
    return back.reshape(ROWS, NX * HEADS * HEAD)


def solution(mesh):
    grid = Mesh(mesh.devices.reshape(NX, NZ, NC, mesh.devices.shape[1]), ("x", "z", "core", "rep"))
    fsdp = ("x", "z", "core")
    whole = P(("rep",) + fsdp, None)
    placed = (whole, whole, P(), P(), P(), P(fsdp, None), P(fsdp, None), P("rep"), P("rep"))
    return jax.shard_map(
        per_device, mesh=grid, in_specs=placed, out_specs=whole, check_vma=False
    )
```

time: 208 us -> 152 us (0.73)
  waiting for transfers between devices: 68.6 us -> 34.9 us
  Pallas kernels: 35.1 us -> 23.9 us
  local copies, waits for them, and re-layouts: 14.6 us -> 3.76 us
  other arithmetic: 10.4 us -> 4.58 us
  starting transfers between devices: 44.3 us -> 49.8 us
    all_to_all x1 -> x0, waiting for transfers between devices: 23.2 us -> none  [per_device(): piece = lax.all_to_all(packed, 'x', split_axis=0, concat_axis=0, tiled=True)]
    ppermute x13 -> x19, waiting for transfers between devices: 40 us -> 27.9 us  [shift(): lax.ppermute(value, axis, [(i, (i + by) % size) for i in range(size)])]
    pallas_call x3 -> x6, Pallas kernels: 35.1 us -> 23.9 us  [the longest x1 7.09 us: per_device(): pl.pallas_call(first_kernel, in_specs=[smem] + [vmem] * 6 + [anywhere] *...]
    ppermute x13 -> x19, starting transfers between devices: 21.5 us -> 32.1 us  [shift(): lax.ppermute(value, axis, [(i, (i + by) % size) for i in range(size)])]
    unnamed x27 -> x21, local copies, waits for them, and re-layouts: 6 us -> 0.08 us
    all_to_all x1 -> x0, starting transfers between devices: 3.48 us -> none  [per_device(): piece = lax.all_to_all(packed, 'x', split_axis=0, concat_axis=0, tiled=True)]
    slice x4 -> x2, local copies, waits for them, and re-layouts: 2.9 us -> 0.01 us  [the longest x1 0.01 us: per_device(): last_b = shift(down[half:], 'z', NZ, -1)]
  transfers between devices with their start and end apart: 16 -> 21, of which waited for: 9 -> 5; matrix products, arithmetic and copies ran while one was open for 10% -> 4% of each run, Pallas kernels for 6% -> 12%
where the time goes in v1:
time: 152 us
  starting transfers between devices  49.8 us (33%)
  waiting for transfers between devices  34.9 us (23%)
  blocking collectives  34.2 us (23%)
  Pallas kernels  23.9 us (16%)
  other arithmetic  4.58 us (3%)
  local copies, waits for them, and re-layouts  3.76 us (2%)
    all_to_all x1, blocking collectives, per_device(): lax.all_to_all(mixed.reshape(NF, RNG, HEADS * HEAD), fsdp, split_axis=0,...  34.2 us
    ppermute x19, starting transfers between devices, shift(): lax.ppermute(value, axis, [(i, (i + by) % size) for i in range(size)])  32.1 us
    ppermute x19, waiting for transfers between devices, shift(): lax.ppermute(value, axis, [(i, (i + by) % size) for i in range(size)])  27.9 us
    all_to_all x1, starting transfers between devices, per_device(): got = lax.all_to_all(sent, fsdp, split_axis=0, concat_axis=0, tiled=True)  11.7 us
    pallas_call x1, Pallas kernels, per_device(): pl.pallas_call(first_kernel, in_specs=[smem] + [vmem] * 6 + [anywhere] *...  7.09 us
    all_to_all x1, waiting for transfers between devices, per_device(): lax.all_to_all(made_kv, ('z', 'core'), split_axis=0, concat_axis=0, tiled...  7.04 us
    pallas_call x1, Pallas kernels, per_device(): pl.pallas_call(prepare_kernel, in_specs=[vmem] * 4, out_specs=vmem, out_s...  6.88 us
    all_to_all x1, starting transfers between devices, per_device(): lax.all_to_all(made_kv, ('z', 'core'), split_axis=0, concat_axis=0, tiled...  6.04 us
  transfers between devices with their start and end apart: 21, of which 5 were waited for; matrix products, arithmetic and copies ran while one was open for 4% of the time, Pallas kernels for 12%

profile of v1, /device:TPU:1, one launch (start us, length us, event | category | flops | bytes accessed | tf_op | source)
XLA Modules:
  0.0 151.5 jit_solution(16682818731053339086)
XLA Ops:
  0.0 0.6 pad_add_fusion.place
  0.6 1.7 %pack_weights.1 = (bf16[80,256]{1,0:T(8,128)(2,1)}, bf16[80,256]{1,0:T(8,128)(2,1)}, bf16[80,256]{1,0:T(8,128)(2,1)}, bf16[80,256]{1,0:T(8,128)(2,1)}) custom-call(s32[3]{0:T(128)} %pad_add_fusion.place, bf16[80,512]{1,0:T(8,128)(2,1)} %key.1, bf16[80,512]{1,0:T(8,128)(2,1)} %value.1), custom_call_target="tpu_custom_call" | custom-call | tf_op jit(solution)/shard_map/pack_weights/pallas_call | solution.py:211
  2.2 3.3 %collective-permute-start.1 = (bf16[80,256]{1,0:T(8,128)(2,1)}, bf16[80,256]{1,0:T(8,128)(2,1)S(1)}, u32[]{:S(2)}, u32[]{:S(2)}) collective-permute-start(bf16[80,256]{1,0:T(8,128)(2,1)} %get-tuple-element.19), channel_id=1, source_target_pairs={{0,192},{64,0},{128,64},{192,128},{1,193},{65,1},{129,65},{193,129... | collective-permute-start | bytes 122888 | tf_op jit(solution)/shard_map/ppermute | solution.py:36
  5.5 0.5 collective-permute-start.2
  6.0 0.6 collective-permute-start
  6.7 2.9 %norm_hidden.1 = (bf16[64,5120]{1,0:T(8,128)(2,1)}, bf16[64,5120]{1,0:T(8,128)(2,1)}) custom-call(bf16[128,5120]{1,0:T(8,128)(2,1)} %hidden.1, f32[1,5120]{1,0:T(1,128)} %bitcast.61), custom_call_target="tpu_custom_call" | custom-call | tf_op jit(solution)/shard_map/norm_hidden/pallas_call | solution.py:223
  9.6 1.5 %collective-permute-start.5 = (bf16[64,5120]{1,0:T(8,128)(2,1)}, bf16[64,5120]{1,0:T(8,128)(2,1)S(1)}, u32[]{:S(2)}, u32[]{:S(2)}) collective-permute-start(bf16[64,5120]{1,0:T(8,128)(2,1)} %get-tuple-element.21.own_a), channel_id=1, source_target_pairs={{0,64},{64,128},{128,192},{192,0},{1,65},{65,129},{129,193},{193,1... | collective-permute-start | bytes 1966088 | tf_op jit(solution)/shard_map/ppermute | solution.py:36
  11.1 1.2 collective-permute-start.6
  12.2 2.3 %copy.15 = bf16[4,16,8,1024]{3,2,1,0:T(8,128)(2,1)} copy(bf16[4,16,8,1024]{3,2,0,1:T(8,128)(2,1)} %bitcast.50) | data formatting | bytes 2097152 | tf_op jit(solution)/shard_map/transpose | solution.py:252
  14.5 11.7 %all-to-all-start = ((bf16[64,8,1024]{2,1,0:T(8,128)(2,1)}), bf16[64,8,1024]{2,1,0:T(8,128)(2,1)S(1)}, u32[]{:S(2)}, u32[]{:S(2)}) async-start(bf16[64,8,1024]{2,1,0:T(8,128)(2,1)} %bitcast.48), calls=%async_computation | async-start | bytes 2097152 | tf_op jit(solution)/shard_map/all_to_all | solution.py:254
  26.3 0.1 add_multiply_fusion.1
  26.4 0.1 add_bitcast_fusion
  26.4 0.2 select_reduce_fusion.2
  26.6 0.1 select_reduce_fusion
  26.8 0.1 subtract_convert_fusion
  26.8 0.0 collective-permute-done.1
  26.8 2.8 %collective-permute-start.10 = (bf16[64,5120]{1,0:T(8,128)(2,1)}, bf16[64,5120]{1,0:T(8,128)(2,1)}, u32[]{:S(2)}, u32[]{:S(2)}) collective-permute-start(bf16[64,5120]{1,0:T(8,128)(2,1)} %get-tuple-element.21.own_a), channel_id=1, source_target_pairs={{0,192},{64,0},{128,64},{192,128},{1,193},{65,1},{129,65},{193,129... | collective-permute-start | bytes 1966088 | tf_op jit(solution)/shard_map/ppermute | solution.py:36
  29.7 0.0 collective-permute-done.2
  29.7 0.0 collective-permute-done
  29.7 1.3 collective-permute-start.3
  31.0 1.5 collective-permute-start.4
  32.5 0.1 copy.16.start
  32.7 22.7 %collective-permute-done.3 = bf16[4,80,256]{2,1,0:T(8,128)(2,1)S(1)} collective-permute-done((bf16[4,80,256]{2,1,0:T(8,128)(2,1)S(1)}, bf16[4,80,256]{2,1,0:T(8,128)(2,1)S(1)}, u32[]{:S(2)}, u32[]{:S(2)}) %collective-permute-start.3) | collective-permute-done | bytes 163872 | tf_op jit(solution)/shard_map/ppermute | solution.py:36
  55.4 1.3 collective-permute-start.9
  56.6 0.0 collective-permute-done.4
  56.7 0.0 collective-permute-done.5.left_a
  56.7 0.0 collective-permute-done.6.right_b
  56.7 0.1 collective-permute-start.11
  56.8 2.7 %collective-permute-start.12 = (bf16[4,80,256]{2,1,0:T(8,128)(2,1)S(1)}, bf16[4,80,256]{2,1,0:T(8,128)(2,1)S(1)}, u32[]{:S(2)}, u32[]{:S(2)}) collective-permute-start(bf16[4,80,256]{2,1,0:T(8,128)(2,1)S(1)} %collective-permute-done.4), channel_id=1, source_target_pairs={{0,56},{8,0},{16,8},{24,16},{32,24},{40,32},{48,40},{56,48},{1,57}... | collective-permute-start | bytes 491528 | tf_op jit(solution)/shard_map/ppermute | solution.py:36
  59.5 0.0 copy-start.2
  59.5 3.0 %collective-permute-done.11 = bf16[4,80,256]{2,1,0:T(8,128)(2,1)S(1)} collective-permute-done((bf16[4,80,256]{2,1,0:T(8,128)(2,1)S(1)}, bf16[4,80,256]{2,1,0:T(8,128)(2,1)S(1)}, u32[]{:S(2)}, u32[]{:S(2)}) %collective-permute-start.11) | collective-permute-done | bytes 163872 | tf_op jit(solution)/shard_map/ppermute | solution.py:36
  62.5 0.0 collective-permute-start.13
  62.5 2.7 %collective-permute-start.14 = (bf16[4,80,256]{2,1,0:T(8,128)(2,1)S(1)}, bf16[4,80,256]{2,1,0:T(8,128)(2,1)S(1)}, u32[]{:S(2)}, u32[]{:S(2)}) collective-permute-start(bf16[4,80,256]{2,1,0:T(8,128)(2,1)S(1)} %collective-permute-done.12), channel_id=1, source_target_pairs={{0,56},{8,0},{16,8},{24,16},{32,24},{40,32},{48,40},{56,48},{1,57}... | collective-permute-start | bytes 491528 | tf_op jit(solution)/shard_map/ppermute | solution.py:36
  65.2 2.9 %collective-permute-start.17 = (bf16[5,4,80,256]{3,2,1,0:T(8,128)(2,1)S(1)}, bf16[5,4,80,256]{3,2,1,0:T(8,128)(2,1)S(1)}, u32[]{:S(2)}, u32[]{:S(2)}) collective-permute-start(bf16[5,4,80,256]{3,2,1,0:T(8,128)(2,1)S(1)} %bitcast_dynamic-update-slice_fusion.mine), channel_id=1, source_target_pairs={{0,4},{4,0},{1,5},{5,1},{2,6},{6,2},{3,7},{7,3},{8,12},{12,8},{9,1... | collective-permute-start | bytes 2457608 | tf_op jit(solution)/shard_map/ppermute | solution.py:36
  68.1 0.1 collective-permute-done.13
  68.2 0.1 collective-permute-start.15
  68.2 0.0 collective-permute-done.14
  68.3 2.7 %collective-permute-start.16 = (bf16[2,80,256]{2,1,0:T(8,128)(2,1)S(1)}, bf16[2,80,256]{2,1,0:T(8,128)(2,1)S(1)}, u32[]{:S(2)}, u32[]{:S(2)}) collective-permute-start(bf16[2,80,256]{2,1,0:T(8,128)(2,1)S(1)} %slice.9), channel_id=1, source_target_pairs={{0,56},{8,0},{16,8},{24,16},{32,24},{40,32},{48,40},{56,48},{1,57}... | collective-permute-start | bytes 245768 | tf_op jit(solution)/shard_map/ppermute | solution.py:36
  71.0 2.0 %collective-permute-done.15 = bf16[2,80,256]{2,1,0:T(8,128)(2,1)S(1)} collective-permute-done((bf16[2,80,256]{2,1,0:T(8,128)(2,1)S(1)}, bf16[2,80,256]{2,1,0:T(8,128)(2,1)S(1)}, u32[]{:S(2)}, u32[]{:S(2)}) %collective-permute-start.15) | collective-permute-done | bytes 81952 | tf_op jit(solution)/shard_map/ppermute | solution.py:36
  73.0 1.0 collective-permute-start.7
  74.0 0.0 collective-permute-done.16
  74.0 1.7 %collective-permute-start.8 = (bf16[64,5120]{1,0:T(8,128)(2,1)S(1)}, bf16[64,5120]{1,0:T(8,128)(2,1)S(1)}, u32[]{:S(2)}, u32[]{:S(2)}) collective-permute-start(bf16[64,5120]{1,0:T(8,128)(2,1)S(1)} %collective-permute-done.6.right_b), channel_id=1, source_target_pairs={{0,192},{64,0},{128,64},{192,128},{1,193},{65,1},{129,65},{193,129... | collective-permute-start | bytes 1966088 | tf_op jit(solution)/shard_map/ppermute | solution.py:36
  75.7 0.1 pad_maximum_fusion.mine2
  75.8 0.0 collective-permute-done.10.right_a
  75.8 4.4 %collective-permute-start.18 = (bf16[3,4,80,256]{3,2,1,0:T(8,128)(2,1)S(1)}, bf16[3,4,80,256]{3,2,1,0:T(8,128)(2,1)S(1)}, u32[]{:S(2)}, u32[]{:S(2)}) collective-permute-start(bf16[3,4,80,256]{3,2,1,0:T(8,128)(2,1)S(1)} %pad_maximum_fusion.mine2), channel_id=1, source_target_pairs={{0,4},{4,0},{1,5},{5,1},{2,6},{6,2},{3,7},{7,3},{8,12},{12,8},{9,1... | collective-permute-start | bytes 1474568 | tf_op jit(solution)/shard_map/ppermute | solution.py:36
  80.2 2.7 %fusion.1 = (f32[512,64]{1,0:T(8,128)S(1)}, f32[512,64]{1,0:T(8,128)S(1)}, f32[512,64]{1,0:T(8,128)S(1)}, f32[512,64]{1,0:T(8,128)}, f32[512,64]{1,0:T(8,128)S(1)}, /*index=5*/f32[512,64]{1,0:T(8,128)}) fusion(f32[64]{0:T(128)S(1)} %negate_power_fusion, f32[512]{0:T(512)S(1)} %get-tuple-element.40, f32[512]{0:T(512)S(1)} %get-tuple-element.41), kind=kLoop, calls=%fused_computation.21 | loop fusion | flops 131072 | bytes 790784 | tf_op jit(solution)/shard_map/neg | solution.py:57
  82.9 0.1 pad_maximum_fusion.3.cosine
  83.0 0.1 pad_maximum_fusion.4.sine
  83.1 0.0 collective-permute-done.9.left_b
  83.2 7.1 %project_first.1 = (f32[3,2,128,128]{3,2,1,0:T(8,128)S(1)}, bf16[4,8,2,80,256]{4,3,2,1,0:T(8,128)(2,1)S(1)}) custom-call(s32[3]{0:T(128)S(1)} %copy-done.1, bf16[64,5120]{1,0:T(8,128)(2,1)} %get-tuple-element.21.own_a, bf16[64,5120]{1,0:T(8,128)(2,1)S(1)} %copy-done, bf16[64,5120]{1,0:T(8,128)(2,1)S(1)} %collective-permute-done.5.left_a, ...), custom_call_target="tpu_custom_call" | custom-call | tf_op jit(solution)/shard_map/project_first/pallas_call | solution.py:282
  90.3 0.0 collective-permute-done.7.far_a
  90.3 0.0 copy-start.3
  90.4 1.5 project_last.1
  91.8 0.0 all-to-all-done
  91.8 6.0 %all-to-all-start.1 = ((bf16[16,48,256]{2,1,0:T(8,128)(2,1)}), bf16[16,48,256]{2,1,0:T(8,128)(2,1)S(1)}, u32[]{:S(2)}, u32[]{:S(2)}) async-start(bf16[16,48,256]{2,1,0:T(8,128)(2,1)} %project_last.1), calls=%async_computation.1 | async-start | bytes 786432 | tf_op jit(solution)/shard_map/all_to_all | solution.py:321
  97.9 0.1 broadcast_add_fusion
  98.0 0.2 add.186.key_token
  98.2 0.1 pad_maximum_fusion.1.cosine
  98.3 0.1 pad_maximum_fusion.2.sine
  98.5 6.9 %prepare_queries.1.q = bf16[4,1024,128]{2,1,0:T(8,128)(2,1)S(1)} custom-call(bf16[512,1024]{1,0:T(8,128)(2,1)S(1)} %bitcast.44, f32[1,128]{1,0:T(1,128)S(1)} %bitcast.47, f32[512,128]{1,0:T(8,128)S(1)} %pad_maximum_fusion.1.cosine, f32[512,128]{1,0:T(8,128)S(1)} %pad_maximum_fusion.2.sine), custom_call_target="tpu_custom_call" | custom-call | tf_op jit(solution)/shard_map/prepare_queries/pallas_call | solution.py:270
  105.4 7.0 %all-to-all-done.1.kv = bf16[16,48,256]{2,1,0:T(8,128)(2,1)S(1)} async-done(((bf16[16,48,256]{2,1,0:T(8,128)(2,1)}), bf16[16,48,256]{2,1,0:T(8,128)(2,1)S(1)}, u32[]{:S(2)}, u32[]{:S(2)}) %all-to-all-start.1) | async-done | bytes 393248 | tf_op jit(solution)/shard_map/all_to_all | solution.py:321
  112.4 3.9 %attend.1 = bf16[512,1024]{1,0:T(8,128)(2,1)S(1)} custom-call(bf16[4,1024,128]{2,1,0:T(8,128)(2,1)S(1)} %prepare_queries.1.q, bf16[16,48,256]{2,1,0:T(8,128)(2,1)S(1)} %all-to-all-done.1.kv, s32[512,1]{1,0:T(8,128)S(1)} %iota_add_fusion.token, s32[512,1]{1,0:T(8,128)S(1)} %copy.16.start, s32[1,768]{1,0:T(1,128)S(1)} %add.186.key_token), custom_call_target="tpu_custom_call" | custom-call | tf_op jit(solution)/shard_map/attend/pallas_call | solution.py:323
  116.3 34.2 %all_to_all.15 = bf16[64,8,1024]{2,1,0:T(8,128)(2,1)S(1)} all-to-all(bf16[64,8,1024]{2,1,0:T(8,128)(2,1)S(1)} %bitcast.43), channel_id=1, replica_groups=mesh['x'=4,'z'=8,'core'=2,'rep'=4] {'x','z','core'}, dimensions={0} | all-to-all | bytes 2097152 | tf_op jit(solution)/shard_map/all_to_all | solution.py:339
  150.5 1.1 copy.17
  (35 shorter events, 0.2 us)
Async XLA Ops:
  2.2 24.6 %collective-permute-start.1 = (bf16[80,256]{1,0:T(8,128)(2,1)}, bf16[80,256]{1,0:T(8,128)(2,1)S(1)}, u32[]{:S(2)}, u32[]{:S(2)}) collective-permute-start(bf16[80,256]{1,0:T(8,128)(2,1)} %get-tuple-element.19), channel_id=1, source_target_pairs={{0,192},{64,0},{128,64},{192,128},{1,193},{65,1},{129,65},{193,129... | collective-permute-start | bytes 122888 | tf_op jit(solution)/shard_map/ppermute | solution.py:36
  5.5 24.2 %collective-permute-start.2 = (bf16[80,256]{1,0:T(8,128)(2,1)}, bf16[80,256]{1,0:T(8,128)(2,1)S(1)}, u32[]{:S(2)}, u32[]{:S(2)}) collective-permute-start(bf16[80,256]{1,0:T(8,128)(2,1)} %get-tuple-element.20), channel_id=1, source_target_pairs={{0,128},{64,192},{128,0},{192,64},{1,129},{65,193},{129,1},{193,65... | collective-permute-start | bytes 122888 | tf_op jit(solution)/shard_map/ppermute | solution.py:36
  6.0 23.6 %collective-permute-start = (bf16[80,256]{1,0:T(8,128)(2,1)}, bf16[80,256]{1,0:T(8,128)(2,1)S(1)}, u32[]{:S(2)}, u32[]{:S(2)}) collective-permute-start(bf16[80,256]{1,0:T(8,128)(2,1)} %get-tuple-element.18), channel_id=1, source_target_pairs={{0,64},{64,128},{128,192},{192,0},{1,65},{65,129},{129,193},{193,1... | collective-permute-start | bytes 122888 | tf_op jit(solution)/shard_map/ppermute | solution.py:36
  6.6 19.8 %copy-start.7 = (s32[64]{0:T(128)S(1)}, s32[64]{0:T(128)}, u32[]{:S(2)}) copy-start(s32[64]{0:T(128)} %param.17) | copy-start | bytes 772
  6.6 19.8 %copy-start.8 = (s32[64]{0:T(128)S(1)}, s32[64]{0:T(128)}, u32[]{:S(2)}) copy-start(s32[64]{0:T(128)} %param.16) | copy-start | bytes 772
  6.6 23.0 %copy-start.6 = (bf16[80,256]{1,0:T(8,128)(2,1)S(1)}, bf16[80,256]{1,0:T(8,128)(2,1)}, u32[]{:S(2)}) copy-start(bf16[80,256]{1,0:T(8,128)(2,1)} %get-tuple-element.17) | copy-start | bytes 122884
  9.6 47.1 %collective-permute-start.5 = (bf16[64,5120]{1,0:T(8,128)(2,1)}, bf16[64,5120]{1,0:T(8,128)(2,1)S(1)}, u32[]{:S(2)}, u32[]{:S(2)}) collective-permute-start(bf16[64,5120]{1,0:T(8,128)(2,1)} %get-tuple-element.21.own_a), channel_id=1, source_target_pairs={{0,64},{64,128},{128,192},{192,0},{1,65},{65,129},{129,193},{193,1... | collective-permute-start | bytes 1966088 | tf_op jit(solution)/shard_map/ppermute | solution.py:36
  11.1 45.6 %collective-permute-start.6 = (bf16[64,5120]{1,0:T(8,128)(2,1)}, bf16[64,5120]{1,0:T(8,128)(2,1)S(1)}, u32[]{:S(2)}, u32[]{:S(2)}) collective-permute-start(bf16[64,5120]{1,0:T(8,128)(2,1)} %get-tuple-element.22.own_b), channel_id=1, source_target_pairs={{0,192},{64,0},{128,64},{192,128},{1,193},{65,1},{129,65},{193,129... | collective-permute-start | bytes 1966088 | tf_op jit(solution)/shard_map/ppermute | solution.py:36
  14.5 77.3 %all-to-all-start = ((bf16[64,8,1024]{2,1,0:T(8,128)(2,1)}), bf16[64,8,1024]{2,1,0:T(8,128)(2,1)S(1)}, u32[]{:S(2)}, u32[]{:S(2)}) async-start(bf16[64,8,1024]{2,1,0:T(8,128)(2,1)} %bitcast.48), calls=%async_computation | async-start | bytes 2097152 | tf_op jit(solution)/shard_map/all_to_all | solution.py:254
  26.8 49.0 %collective-permute-start.10 = (bf16[64,5120]{1,0:T(8,128)(2,1)}, bf16[64,5120]{1,0:T(8,128)(2,1)}, u32[]{:S(2)}, u32[]{:S(2)}) collective-permute-start(bf16[64,5120]{1,0:T(8,128)(2,1)} %get-tuple-element.21.own_a), channel_id=1, source_target_pairs={{0,192},{64,0},{128,64},{192,128},{1,193},{65,1},{129,65},{193,129... | collective-permute-start | bytes 1966088 | tf_op jit(solution)/shard_map/ppermute | solution.py:36
  29.7 25.7 %collective-permute-start.3 = (bf16[4,80,256]{2,1,0:T(8,128)(2,1)S(1)}, bf16[4,80,256]{2,1,0:T(8,128)(2,1)S(1)}, u32[]{:S(2)}, u32[]{:S(2)}) collective-permute-start(bf16[4,80,256]{2,1,0:T(8,128)(2,1)S(1)} %pad_maximum_fusion.5), channel_id=1, source_target_pairs={{0,8},{8,16},{16,24},{24,32},{32,40},{40,48},{48,56},{56,0},{1,9},... | collective-permute-start | bytes 491528 | tf_op jit(solution)/shard_map/ppermute | solution.py:36
  31.0 25.7 %collective-permute-start.4 = (bf16[4,80,256]{2,1,0:T(8,128)(2,1)S(1)}, bf16[4,80,256]{2,1,0:T(8,128)(2,1)S(1)}, u32[]{:S(2)}, u32[]{:S(2)}) collective-permute-start(bf16[4,80,256]{2,1,0:T(8,128)(2,1)S(1)} %pad_maximum_fusion.5), channel_id=1, source_target_pairs={{0,56},{8,0},{16,8},{24,16},{32,24},{40,32},{48,40},{56,48},{1,57}... | collective-permute-start | bytes 491528 | tf_op jit(solution)/shard_map/ppermute | solution.py:36
  55.4 27.8 %collective-permute-start.9 = (bf16[64,5120]{1,0:T(8,128)(2,1)}, bf16[64,5120]{1,0:T(8,128)(2,1)S(1)}, u32[]{:S(2)}, u32[]{:S(2)}) collective-permute-start(bf16[64,5120]{1,0:T(8,128)(2,1)} %get-tuple-element.22.own_b), channel_id=1, source_target_pairs={{0,64},{64,128},{128,192},{192,0},{1,65},{65,129},{129,193},{193,1... | collective-permute-start | bytes 1966088 | tf_op jit(solution)/shard_map/ppermute | solution.py:36
  56.7 5.8 %collective-permute-start.11 = (bf16[4,80,256]{2,1,0:T(8,128)(2,1)S(1)}, bf16[4,80,256]{2,1,0:T(8,128)(2,1)S(1)}, u32[]{:S(2)}, u32[]{:S(2)}) collective-permute-start(bf16[4,80,256]{2,1,0:T(8,128)(2,1)S(1)} %collective-permute-done.3), channel_id=1, source_target_pairs={{0,8},{8,16},{16,24},{24,32},{32,40},{40,48},{48,56},{56,0},{1,9},... | collective-permute-start | bytes 491528 | tf_op jit(solution)/shard_map/ppermute | solution.py:36
  56.8 5.7 %collective-permute-start.12 = (bf16[4,80,256]{2,1,0:T(8,128)(2,1)S(1)}, bf16[4,80,256]{2,1,0:T(8,128)(2,1)S(1)}, u32[]{:S(2)}, u32[]{:S(2)}) collective-permute-start(bf16[4,80,256]{2,1,0:T(8,128)(2,1)S(1)} %collective-permute-done.4), channel_id=1, source_target_pairs={{0,56},{8,0},{16,8},{24,16},{32,24},{40,32},{48,40},{56,48},{1,57}... | collective-permute-start | bytes 491528 | tf_op jit(solution)/shard_map/ppermute | solution.py:36
  59.5 23.7 %copy-start = (bf16[64,5120]{1,0:T(8,128)(2,1)S(1)}, bf16[64,5120]{1,0:T(8,128)(2,1)}, u32[]{:S(2)}) copy-start(bf16[64,5120]{1,0:T(8,128)(2,1)} %get-tuple-element.22.own_b) | copy-start | bytes 1966084
  59.5 23.7 %copy-start.1 = (s32[3]{0:T(128)S(1)}, s32[3]{0:T(128)}, u32[]{:S(2)}) copy-start(s32[3]{0:T(128)} %pad_add_fusion.place) | copy-start | bytes 40
  59.5 23.7 %copy-start.2 = (f32[128]{0:T(128)S(1)}, f32[128]{0:T(128)}, u32[]{:S(2)}) copy-start(f32[128]{0:T(128)} %param.13) | copy-start | bytes 1540
  62.5 5.7 %collective-permute-start.13 = (bf16[4,80,256]{2,1,0:T(8,128)(2,1)S(1)}, bf16[4,80,256]{2,1,0:T(8,128)(2,1)S(1)}, u32[]{:S(2)}, u32[]{:S(2)}) collective-permute-start(bf16[4,80,256]{2,1,0:T(8,128)(2,1)S(1)} %collective-permute-done.11), channel_id=1, source_target_pairs={{0,8},{8,16},{16,24},{24,32},{32,40},{40,48},{48,56},{56,0},{1,9},... | collective-permute-start | bytes 491528 | tf_op jit(solution)/shard_map/ppermute | solution.py:36
  62.5 5.8 %collective-permute-start.14 = (bf16[4,80,256]{2,1,0:T(8,128)(2,1)S(1)}, bf16[4,80,256]{2,1,0:T(8,128)(2,1)S(1)}, u32[]{:S(2)}, u32[]{:S(2)}) collective-permute-start(bf16[4,80,256]{2,1,0:T(8,128)(2,1)S(1)} %collective-permute-done.12), channel_id=1, source_target_pairs={{0,56},{8,0},{16,8},{24,16},{32,24},{40,32},{48,40},{56,48},{1,57}... | collective-permute-start | bytes 491528 | tf_op jit(solution)/shard_map/ppermute | solution.py:36
  65.2 18.0 %collective-permute-start.17 = (bf16[5,4,80,256]{3,2,1,0:T(8,128)(2,1)S(1)}, bf16[5,4,80,256]{3,2,1,0:T(8,128)(2,1)S(1)}, u32[]{:S(2)}, u32[]{:S(2)}) collective-permute-start(bf16[5,4,80,256]{3,2,1,0:T(8,128)(2,1)S(1)} %bitcast_dynamic-update-slice_fusion.mine), channel_id=1, source_target_pairs={{0,4},{4,0},{1,5},{5,1},{2,6},{6,2},{3,7},{7,3},{8,12},{12,8},{9,1... | collective-permute-start | bytes 2457608 | tf_op jit(solution)/shard_map/ppermute | solution.py:36
  68.2 4.9 %collective-permute-start.15 = (bf16[2,80,256]{2,1,0:T(8,128)(2,1)S(1)}, bf16[2,80,256]{2,1,0:T(8,128)(2,1)S(1)}, u32[]{:S(2)}, u32[]{:S(2)}) collective-permute-start(bf16[2,80,256]{2,1,0:T(8,128)(2,1)S(1)} %slice.8), channel_id=1, source_target_pairs={{0,8},{8,16},{16,24},{24,32},{32,40},{40,48},{48,56},{56,0},{1,9},... | collective-permute-start | bytes 245768 | tf_op jit(solution)/shard_map/ppermute | solution.py:36
  68.3 5.7 %collective-permute-start.16 = (bf16[2,80,256]{2,1,0:T(8,128)(2,1)S(1)}, bf16[2,80,256]{2,1,0:T(8,128)(2,1)S(1)}, u32[]{:S(2)}, u32[]{:S(2)}) collective-permute-start(bf16[2,80,256]{2,1,0:T(8,128)(2,1)S(1)} %slice.9), channel_id=1, source_target_pairs={{0,56},{8,0},{16,8},{24,16},{32,24},{40,32},{48,40},{56,48},{1,57}... | collective-permute-start | bytes 245768 | tf_op jit(solution)/shard_map/ppermute | solution.py:36
  73.0 17.3 %collective-permute-start.7 = (bf16[64,5120]{1,0:T(8,128)(2,1)S(1)}, bf16[64,5120]{1,0:T(8,128)(2,1)S(1)}, u32[]{:S(2)}, u32[]{:S(2)}) collective-permute-start(bf16[64,5120]{1,0:T(8,128)(2,1)S(1)} %collective-permute-done.5.left_a), channel_id=1, source_target_pairs={{0,64},{64,128},{128,192},{192,0},{1,65},{65,129},{129,193},{193,1... | collective-permute-start | bytes 1966088 | tf_op jit(solution)/shard_map/ppermute | solution.py:36
  74.0 16.3 %collective-permute-start.8 = (bf16[64,5120]{1,0:T(8,128)(2,1)S(1)}, bf16[64,5120]{1,0:T(8,128)(2,1)S(1)}, u32[]{:S(2)}, u32[]{:S(2)}) collective-permute-start(bf16[64,5120]{1,0:T(8,128)(2,1)S(1)} %collective-permute-done.6.right_b), channel_id=1, source_target_pairs={{0,192},{64,0},{128,64},{192,128},{1,193},{65,1},{129,65},{193,129... | collective-permute-start | bytes 1966088 | tf_op jit(solution)/shard_map/ppermute | solution.py:36
  75.8 7.3 %collective-permute-start.18 = (bf16[3,4,80,256]{3,2,1,0:T(8,128)(2,1)S(1)}, bf16[3,4,80,256]{3,2,1,0:T(8,128)(2,1)S(1)}, u32[]{:S(2)}, u32[]{:S(2)}) collective-permute-start(bf16[3,4,80,256]{3,2,1,0:T(8,128)(2,1)S(1)} %pad_maximum_fusion.mine2), channel_id=1, source_target_pairs={{0,4},{4,0},{1,5},{5,1},{2,6},{6,2},{3,7},{7,3},{8,12},{12,8},{9,1... | collective-permute-start | bytes 1474568 | tf_op jit(solution)/shard_map/ppermute | solution.py:36
  90.3 7.9 %copy-start.5 = (f32[512,64]{1,0:T(8,128)S(1)}, f32[512,64]{1,0:T(8,128)}, u32[]{:S(2)}) copy-start(f32[512,64]{1,0:T(8,128)} %get-tuple-element.37) | copy-start | bytes 393220
  90.3 8.0 %copy-start.4 = (f32[512,64]{1,0:T(8,128)S(1)}, f32[512,64]{1,0:T(8,128)}, u32[]{:S(2)}) copy-start(f32[512,64]{1,0:T(8,128)} %get-tuple-element.39) | copy-start | bytes 393220
  90.3 8.1 %copy-start.3 = (f32[128]{0:T(128)S(1)}, f32[128]{0:T(128)}, u32[]{:S(2)}) copy-start(f32[128]{0:T(128)} %param.12) | copy-start | bytes 1540
  91.8 20.6 %all-to-all-start.1 = ((bf16[16,48,256]{2,1,0:T(8,128)(2,1)}), bf16[16,48,256]{2,1,0:T(8,128)(2,1)S(1)}, u32[]{:S(2)}, u32[]{:S(2)}) async-start(bf16[16,48,256]{2,1,0:T(8,128)(2,1)} %project_last.1), calls=%async_computation.1 | async-start | bytes 786432 | tf_op jit(solution)/shard_map/all_to_all | solution.py:321
